TPU v7x, 32 devices: a whole 2x2x4 slice. The times are simulated.
32 devices in a mesh: exp: 8 (over z, y), row: 4 (over x, core).
Axes of the slice: x: 2, y: 2, z: 4, core: 2. Of those that a mesh axis runs over, the one named last changes fastest.
Arguments:
- latent: bfloat16 [4, 1024, 1024], P(None, 'row', 'exp'), may hold values from -6 to 6
- row_taps: bfloat16 [16, 21], replicated, may hold values from -1.25 to 1.25
- column_taps: bfloat16 [16, 21], replicated, may hold values from -1.25 to 1.25
- coefficients: bfloat16 [8, 16, 1024, 1024], P('exp', None, 'row'), may hold values from -1.5 to 1.5
- observed: bfloat16 [8, 1024, 1024], P('exp', 'row'), may hold values from -6 to 6
- cell_of: int32 [8, 1], replicated, may hold values from 0 to 3
- valid_rows: int32 [8, 1024], P('exp', 'row'), may hold values 0 or 1
Outputs:
- gradient: float32 [4, 1024, 1024], P(None, 'row', 'exp')
- residuals: float32 [8, 1024, 1024], P('exp', 'row')
Inputs may be any that keep to these rules, and one draw needn't show every extreme that they name: `cell_of`: every sky cell is covered by at least one exposure.
All inputs are finite; a program needn't handle non-finite values. No bound on the sum of `valid_rows` on one device may be relied on, other than what follows from the above.
Results may differ from a plain program's by a relative error of at most 0.0023.
Values may be sent and summed in bfloat16 or wider, within the bound.
A program may use at most 128 MiB of HBM per device.

v0:
```python
import functools

import jax
import jax.numpy as jnp
from jax import lax
from jax.experimental import pallas as pl
from jax.experimental.pallas import tpu as pltpu
from jax.sharding import PartitionSpec as P

LANES = 128
WINDOW = 256
PACK = 16
STEP = 64
MESH = pl.DeviceIdType.MESH


def round_up(value, step):
    return -(-value // step) * step


def from_behind(block, axis, distance):
    devices = range(lax.axis_size(axis))
    route = [(i - distance, i) for i in devices if i - distance in devices]
    return lax.ppermute(block, axis, route)


def toeplitz(taps_row, rows, first):
    parts = []
    for at in range(0, rows, STEP):
        moved = pltpu.roll(jnp.broadcast_to(taps_row, (8, WINDOW)), (first + at) % WINDOW, 1)
        spread = jnp.broadcast_to(moved[:1], (min(STEP, rows - at), WINDOW))
        parts.append(pltpu.roll(spread, 0, 1, stride=1, stride_axis=0))
    return jnp.concatenate(parts, axis=0)


def filters_kernel(
    dims,
    lat_ref, taps_ref, obs_ref, mask_ref, coef_hbm, above_hbm, below_hbm,
    res_ref, term_ref,
    coef, lsh, fw, gw, aw, bw, rb, resid, cb, tsh, sems,
):
    kernels, tap_count, strip, width, inner, outer = dims
    half_width = tap_count // 2
    half = strip // 2
    block = half + inner
    chunks = width // WINDOW

    def copies(c):
        cols = pl.ds(c * WINDOW, WINDOW)
        return (
            pltpu.make_async_copy(
                coef_hbm.at[:, :, cols], coef.at[:, pl.ds(inner, strip), cols], sems.at[c, 0]),
            pltpu.make_async_copy(
                above_hbm.at[:, :, cols], coef.at[:, pl.ds(0, inner), cols], sems.at[c, 1]),
            pltpu.make_async_copy(
                below_hbm.at[:, :, cols], coef.at[:, pl.ds(inner + strip, inner), cols], sems.at[c, 2]),
        )

    for c in range(chunks):
        for copy in copies(c):
            copy.start()

    lsh[:, pl.ds(0, LANES)] = jnp.zeros((lsh.shape[0], LANES), lsh.dtype)
    lsh[:, pl.ds(width, LANES)] = jnp.zeros((lsh.shape[0], LANES), lsh.dtype)
    lsh[:, pl.ds(LANES // 2, width)] = lat_ref[...]

    low_a = strip + 2 * outer - WINDOW
    low_b = strip + 2 * inner - WINDOW
    side = LANES // 2 + half_width

    @pl.loop(0, kernels // 2)
    def _(pair):
        for odd in range(2):
            k = 2 * pair + odd
            row = taps_ref[0, pl.ds(k, 1), :]
            row_rev = taps_ref[1, pl.ds(k, 1), :]
            col = taps_ref[2, pl.ds(k, 1), :]
            col_rev = taps_ref[3, pl.ds(k, 1), :]
            shape = (pl.ds(odd * LANES, LANES))
            fw[pair, :, shape] = toeplitz(row_rev, WINDOW, -side)[:, :LANES].astype(fw.dtype)
            gw[k] = toeplitz(row, WINDOW, -side)[:, :LANES].astype(gw.dtype)
            aw[k, 0] = toeplitz(col, block, outer - inner - half_width).astype(aw.dtype)
            aw[k, 1] = toeplitz(col, block, half + outer - half_width - low_a).astype(aw.dtype)
            bw[k, 0] = toeplitz(col_rev, half, inner - half_width).astype(bw.dtype)
            bw[k, 1] = toeplitz(col_rev, half, half + inner - half_width - low_b).astype(bw.dtype)

    @pl.loop(0, chunks)
    def _(c):
        for copy in copies(c):
            copy.wait()
        start = pl.multiple_of(c * WINDOW, WINDOW)
        cols = pl.ds(start, WINDOW)
        for b in range(WINDOW // LANES):
            window = lsh[:, pl.ds(pl.multiple_of(start + b * LANES, LANES), WINDOW)]
            for pair in range(kernels // 2):
                both = jnp.dot(window, fw[pair], preferred_element_type=jnp.float32).astype(rb.dtype)
                rb[2 * pair, :, pl.ds(b * LANES, LANES)] = both[:, :LANES]
                rb[2 * pair + 1, :, pl.ds(b * LANES, LANES)] = both[:, LANES:]
        for part in range(2):
            rows = pl.ds(part * block, block)
            seen = pl.ds(part * low_a, WINDOW)
            predicted = jnp.zeros((block, WINDOW), jnp.float32)
            for k in range(kernels):
                vertical = jnp.dot(aw[k, part], rb[k, seen, :], preferred_element_type=jnp.float32)
                predicted += coef[k, rows, cols].astype(jnp.float32) * vertical
            mask = mask_ref[rows, :]
            mask = jnp.concatenate([mask] * (WINDOW // LANES), axis=1)
            resid[rows, :] = mask * (predicted - obs_ref[rows, cols].astype(jnp.float32))
        res_ref[:, cols] = resid[pl.ds(inner, strip), :]
        for k in range(kernels):
            weighted = (coef[k, :, cols].astype(jnp.float32) * resid[...]).astype(jnp.bfloat16)
            for part in range(2):
                seen = weighted[part * low_b:part * low_b + WINDOW]
                back = jnp.dot(bw[k, part], seen, preferred_element_type=jnp.float32)
                cb[k, pl.ds(part * half, half), cols] = back.astype(cb.dtype)

    blocks = width // LANES
    for out, source, taps_at in (
        (0, 0, LANES), (width, width - LANES, 0),
    ):
        total = jnp.zeros((strip, LANES), jnp.float32)
        for k in range(kernels):
            total += jnp.dot(
                cb[k, :, pl.ds(source, LANES)], gw[k, pl.ds(taps_at, LANES), :],
                preferred_element_type=jnp.float32)
        tsh[:, pl.ds(out, LANES)] = total

    @pl.loop(0, blocks - 1)
    def _(b):
        source = pl.multiple_of(b * LANES, LANES)
        total = jnp.zeros((strip, LANES), jnp.float32)
        for k in range(kernels):
            total += jnp.dot(
                cb[k, :, pl.ds(source, WINDOW)], gw[k], preferred_element_type=jnp.float32)
        tsh[:, pl.ds(pl.multiple_of(source + LANES, LANES), LANES)] = total

    term_ref[...] = tsh[:, pl.ds(LANES // 2, width)].astype(term_ref.dtype)


def apart_body(latent, row_taps, column_taps, coefficients, observed, cell_of, valid_rows):
    kernels, tap_count = row_taps.shape
    half_width = tap_count // 2
    strip, width = observed.shape[1:]
    ncells = latent.shape[0]
    inner = round_up(half_width, PACK)
    outer = round_up(2 * half_width, PACK)
    cell_list = cell_of[:, 0]

    above_coef = from_behind(coefficients[0, :, strip - inner:], "row", 1)
    below_coef = from_behind(coefficients[0, :, :inner], "row", -1)
    usable = jnp.broadcast_to(valid_rows[0].astype(jnp.bfloat16)[:, None], (strip, LANES))
    seen = jnp.concatenate([observed[0], usable], axis=1)
    seen = jnp.concatenate(
        [from_behind(seen[strip - inner:], "row", 1), seen, from_behind(seen[:inner], "row", -1)], axis=0)
    mask = seen[:, width:].astype(jnp.float32)
    seen = seen[:, :width]

    outgoing = jnp.take(latent, cell_list, axis=0)
    arrived = lax.all_to_all(outgoing, "exp", split_axis=0, concat_axis=2, tiled=True)[0]
    extended = jnp.concatenate(
        [from_behind(arrived[strip - outer:], "row", 1), arrived, from_behind(arrived[:outer], "row", -1)], axis=0)

    taps = jnp.stack([row_taps, row_taps[:, ::-1], column_taps, column_taps[:, ::-1]]).astype(jnp.float32)
    taps = jnp.pad(taps, ((0, 0), (0, 0), (0, WINDOW - tap_count)))

    vmem = pl.BlockSpec(memory_space=pltpu.VMEM)
    hbm = pl.BlockSpec(memory_space=pl.ANY)
    dims = (kernels, tap_count, strip, width, inner, outer)
    block = strip // 2 + inner
    bf16 = jnp.bfloat16
    residual, term = pl.pallas_call(
        functools.partial(filters_kernel, dims),
        out_shape=(
            jax.ShapeDtypeStruct((strip, width), jnp.float32),
            jax.ShapeDtypeStruct((strip, width), bf16),
        ),
        in_specs=[vmem, vmem, vmem, vmem, hbm, hbm, hbm],
        out_specs=(vmem, vmem),
        scratch_shapes=[
            pltpu.VMEM((kernels, strip + 2 * inner, width), bf16),
            pltpu.VMEM((strip + 2 * outer, width + LANES), bf16),
            pltpu.VMEM((kernels // 2, WINDOW, 2 * LANES), bf16),
            pltpu.VMEM((kernels, WINDOW, LANES), bf16),
            pltpu.VMEM((kernels, 2, block, WINDOW), bf16),
            pltpu.VMEM((kernels, 2, strip // 2, WINDOW), bf16),
            pltpu.VMEM((kernels, strip + 2 * outer, WINDOW), bf16),
            pltpu.VMEM((strip + 2 * inner, WINDOW), jnp.float32),
            pltpu.VMEM((kernels, strip, width), bf16),
            pltpu.VMEM((strip, width + LANES), jnp.float32),
            pltpu.SemaphoreType.DMA((width // WINDOW, 3)),
        ],
        compiler_params=pltpu.CompilerParams(vmem_limit_bytes=56 * 2**20),
        cost_estimate=pl.CostEstimate(flops=10**10, bytes_accessed=2 * 10**7, transcendentals=0),
    )(extended, taps, seen, mask, coefficients[0], above_coef, below_coef)

    incoming = lax.all_to_all(term[None], "exp", split_axis=2, concat_axis=0, tiled=True)
    owner = jnp.arange(ncells)[:, None] == cell_list[None, :]
    gradient = jnp.sum(
        jnp.where(owner[:, :, None, None], incoming[None].astype(jnp.float32), 0.0), axis=1)
    return (gradient, residual[None])


def fused_kernel(
    dims,
    cells_hbm, lat_hbm, along_hbm, down_hbm, valid_hbm, obs_hbm, coef_hbm,
    res_ref, grad_ref,
    cells_ref, lat_ref, along_ref, down_ref, valid_ref, cells, taps_ref, coef, seen, usable, outgoing, lat, lsh, fw, gw, ew, aw, bw, resid, tot, stray, leaving, arrived,
    own_sems, lat_send, lat_recv, rim_send, rim_recv, halo_send, halo_recv, term_send, term_recv,
):
    count, row_count, kernels, tap_count, strip, width, inner, outer = dims
    half_width = tap_count // 2
    half = strip // 2
    block = half + inner
    chunks = width // WINDOW
    per = WINDOW // LANES
    me = lax.axis_index("exp")
    row = lax.axis_index("row")
    rising = me < count // 2
    has_above = row > 0
    has_below = row < row_count - 1

    def ordered(rank, length):
        return jnp.where(rising, rank, length - 1 - rank)

    def reversed_order(rank, length):
        return jnp.where(rising, length - 1 - rank, rank)

    def lane_block(b):
        return pl.ds(pl.multiple_of(b * LANES, LANES), LANES)

    def chunk_cols(c):
        return pl.ds(pl.multiple_of(c * WINDOW, WINDOW), WINDOW)

    barrier = pltpu.get_barrier_semaphore()
    for e in range(count):
        @pl.when(e != me)
        def _():
            pl.semaphore_signal(barrier, inc=1, device_id={"exp": e}, device_id_type=MESH)

    @pl.when(has_above)
    def _():
        pl.semaphore_signal(barrier, inc=1, device_id={"row": row - 1}, device_id_type=MESH)

    @pl.when(has_below)
    def _():
        pl.semaphore_signal(barrier, inc=1, device_id={"row": row + 1}, device_id_type=MESH)

    def own_coef(c):
        cols = chunk_cols(c)
        return pltpu.make_async_copy(
            coef_hbm.at[:, :, cols], coef.at[:, pl.ds(inner, strip), cols], own_sems.at[c])

    own_seen = pltpu.make_async_copy(obs_hbm, seen.at[pl.ds(inner, strip)], own_sems.at[chunks])
    fetched = [
        pltpu.make_async_copy(src, dst, own_sems.at[chunks + 1 + i])
        for i, (src, dst) in enumerate((
            (cells_hbm, cells_ref), (lat_hbm, lat_ref), (along_hbm, along_ref),
            (down_hbm, down_ref), (valid_hbm, valid_ref)))]
    for copy in fetched:
        copy.start()
    own_seen.start()
    for step in range(chunks):
        own_coef(ordered(step, chunks)).start()

    for copy in fetched:
        copy.wait()
    for e in range(count):
        cells[e] = jnp.broadcast_to(cells_ref[:, e:e + 1], (8, LANES))

    def owned(e, c):
        return jnp.concatenate([(cells[e] == c).astype(jnp.float32)] * (strip // 8), axis=0) > 0.5

    for e in range(count):
        chosen = lat_ref[0].astype(jnp.float32)
        for c in range(1, lat_ref.shape[0]):
            chosen = jnp.where(owned(e, c), lat_ref[c].astype(jnp.float32), chosen)
        outgoing[e] = chosen.astype(outgoing.dtype)
    at_row = lax.broadcasted_iota(jnp.int32, (strip, strip), 0)
    at_col = lax.broadcasted_iota(jnp.int32, (strip, strip), 1)
    spread = jnp.where(at_row == at_col, valid_ref[...], 0).astype(jnp.bfloat16)
    usable[pl.ds(inner, strip), :] = jnp.dot(
        spread, jnp.ones((strip, LANES), jnp.bfloat16),
        preferred_element_type=jnp.float32).astype(usable.dtype)
    for ref in (lat,):
        ref[:, pl.ds(0, LANES)] = jnp.zeros((ref.shape[0], LANES), ref.dtype)
        ref[:, pl.ds(LANES + width, LANES)] = jnp.zeros((ref.shape[0], LANES), ref.dtype)

    def fill(at_lat, at_inner):
        lat[pl.ds(at_lat, outer), :] = jnp.zeros((outer, lat.shape[1]), lat.dtype)
        coef[:, pl.ds(at_inner, inner), :] = jnp.zeros((kernels, inner, width), coef.dtype)
        seen[pl.ds(at_inner, inner), :] = jnp.zeros((inner, width), seen.dtype)
        usable[pl.ds(at_inner, inner), :] = jnp.zeros((inner, LANES), usable.dtype)

    @pl.when(jnp.logical_not(has_above))
    def _():
        fill(0, 0)

    @pl.when(jnp.logical_not(has_below))
    def _():
        fill(outer + strip, inner + strip)

    pl.semaphore_wait(barrier, count - 1 + has_above.astype(jnp.int32) + has_below.astype(jnp.int32))

    strip_rows = pl.ds(outer, strip)

    def lat_copy(e):
        return pltpu.make_async_remote_copy(
            src_ref=outgoing.at[e], dst_ref=lat.at[strip_rows, lane_block(me + 1)],
            send_sem=lat_send.at[e], recv_sem=lat_recv.at[me],
            device_id={"exp": e}, device_id_type=MESH)

    def own_lat():
        return pltpu.make_async_copy(
            outgoing.at[me], lat.at[strip_rows, lane_block(me + 1)], lat_recv.at[me])

    def halo_copies(c, side):
        cols = chunk_cols(c)
        source = pl.ds(0 if side == 0 else strip - inner, inner)
        target = pl.ds(inner + strip if side == 0 else 0, inner)
        return pltpu.make_async_remote_copy(
            src_ref=coef_hbm.at[:, source, cols], dst_ref=coef.at[:, target, cols],
            send_sem=halo_send.at[side, c], recv_sem=halo_recv.at[side, c],
            device_id={"row": row - 1 if side == 0 else row + 1}, device_id_type=MESH)

    def seen_copies(side):
        source = 0 if side == 0 else strip - inner
        target = pl.ds(inner + strip if side == 0 else 0, inner)
        return [pltpu.make_async_remote_copy(
            src_ref=src.at[pl.ds(first + source, inner)], dst_ref=dst.at[target],
            send_sem=halo_send.at[side, chunks + i], recv_sem=halo_recv.at[side, chunks + i],
            device_id={"row": row - 1 if side == 0 else row + 1}, device_id_type=MESH)
            for i, (src, first, dst) in enumerate(((obs_hbm, 0, seen), (usable, inner, usable)))]

    def rim_copy(b, side):
        cols = lane_block(b + 1)
        source = pl.ds(outer if side == 0 else strip, outer)
        target = pl.ds(outer + strip if side == 0 else 0, outer)
        return pltpu.make_async_remote_copy(
            src_ref=lat.at[source, cols], dst_ref=lat.at[target, cols],
            send_sem=rim_send.at[side, b], recv_sem=rim_recv.at[side, b],
            device_id={"row": row - 1 if side == 0 else row + 1}, device_id_type=MESH)

    sends = ((0, has_above), (1, has_below))
    receives = ((0, has_below), (1, has_above))

    def start_halos(step):
        for side, there in sends:
            @pl.when(there)
            def _():
                halo_copies(ordered(step, chunks), side).start()

    late = ordered(me, count) < count // 4
    own_lat().start()
    for rank in range(count):
        e = ordered(rank, count)
        @pl.when(jnp.logical_and(e != me, jnp.logical_or(jnp.logical_not(late), rank < count // 2)))
        def _():
            lat_copy(e).start()
    start_halos(0)
    for side, there in sends:
        @pl.when(there)
        def _():
            for copy in seen_copies(side):
                copy.start()

    low_a = strip + 2 * outer - WINDOW
    low_b = strip + 2 * inner - WINDOW
    shift = LANES // 2 + half_width

    at_tap = lax.broadcasted_iota(jnp.int32, (tap_count, WINDOW), 0)
    at_lane = lax.broadcasted_iota(jnp.int32, (tap_count, WINDOW), 1)
    keep = (at_tap == at_lane).astype(jnp.float32).astype(jnp.bfloat16)
    turn = (at_tap + at_lane == tap_count - 1).astype(jnp.float32).astype(jnp.bfloat16)
    for i, (taps, order) in enumerate(((along_ref, keep), (along_ref, turn), (down_ref, keep), (down_ref, turn))):
        taps_ref[i] = jnp.dot(taps[...], order, preferred_element_type=jnp.float32)

    far = (
        lax.broadcasted_iota(jnp.int32, (WINDOW, WINDOW), 0)
        - lax.broadcasted_iota(jnp.int32, (WINDOW, WINDOW), 1))
    corner = jnp.abs(far) >= LANES

    @pl.loop(0, kernels // 2)
    def _(pair):
        for odd in range(2):
            k = 2 * pair + odd
            along = taps_ref[0, pl.ds(k, 1), :]
            along_rev = taps_ref[1, pl.ds(k, 1), :]
            down = taps_ref[2, pl.ds(k, 1), :]
            down_rev = taps_ref[3, pl.ds(k, 1), :]
            fw[pair, :, pl.ds(odd * LANES, LANES)] = toeplitz(along_rev, WINDOW, -shift)[:, :LANES].astype(fw.dtype)
            ring = toeplitz(along, WINDOW, -half_width)
            gw[k] = jnp.where(corner, 0.0, ring).astype(gw.dtype)
            reach = jnp.where(corner, ring, 0.0)
            reach = reach[:, :LANES] + reach[:, LANES:]
            ew[pair, pl.ds(odd * LANES, LANES // 2), :] = reach[:LANES // 2].astype(ew.dtype)
            ew[pair, pl.ds(odd * LANES + LANES // 2, LANES // 2), :] = reach[WINDOW - LANES // 2:].astype(ew.dtype)
            aw[k, 0] = toeplitz(down, block, outer - inner - half_width).astype(aw.dtype)
            aw[k, 1] = toeplitz(down, block, half + outer - half_width - low_a).astype(aw.dtype)
            bw[k, 0] = toeplitz(down_rev, half, inner - half_width).astype(bw.dtype)
            bw[k, 1] = toeplitz(down_rev, half, half + inner - half_width - low_b).astype(bw.dtype)

    for at in (0, chunks + 1):
        stray[at] = jnp.zeros((strip, LANES), stray.dtype)

    def take_block(rank):
        b = ordered(rank, count)
        pltpu.make_async_copy(
            outgoing.at[0], lat.at[strip_rows, lane_block(b + 1)], lat_recv.at[b]).wait()
        for side, there in sends:
            @pl.when(there)
            def _():
                rim_copy(b, side).start()

    def take_rims(rank):
        b = ordered(rank, count)
        for side, there in receives:
            @pl.when(there)
            def _():
                rim_copy(b, side).wait_recv()

    for rank in range(count // 2, count):
        @pl.when(late)
        def _():
            lat_copy(ordered(rank, count)).start()
    for rank in range(per + 1):
        take_block(rank)
    own_seen.wait()
    for side, there in receives:
        @pl.when(there)
        def _():
            for copy in seen_copies(side):
                copy.wait_recv()
    take_rims(0)

    @pl.loop(0, chunks)
    def _(step):
        c = ordered(step, chunks)
        cols = chunk_cols(c)

        @pl.when(step + 1 < chunks)
        def _():
            start_halos(step + 1)

        for more in range(1, per + 1):
            @pl.when(step * per + more < count)
            def _():
                take_rims(step * per + more)
        near = lat[:, pl.ds(pl.multiple_of(c * WINDOW, WINDOW), WINDOW + 2 * LANES)]
        lsh[...] = near[:, LANES // 2:LANES // 2 + WINDOW + LANES]
        own_coef(c).wait()
        for side, there in receives:
            @pl.when(there)
            def _():
                halo_copies(c, side).wait_recv()
        windows = [lsh[:, b * LANES:b * LANES + WINDOW] for b in range(per)]

        def predict(pairs, predicted):
            for pair in pairs:
                both = [
                    jnp.dot(window, fw[pair], preferred_element_type=jnp.float32).astype(jnp.bfloat16)
                    for window in windows]
                for odd in range(2):
                    k = 2 * pair + odd
                    blurred = jnp.concatenate(
                        [found[:, odd * LANES:(odd + 1) * LANES] for found in both], axis=1)
                    for part in range(2):
                        vertical = jnp.dot(
                            aw[k, part], blurred[part * low_a:part * low_a + WINDOW],
                            preferred_element_type=jnp.float32)
                        gain = coef[k, pl.ds(part * block, block), cols].astype(jnp.float32)
                        predicted[part] = predicted[part] + gain * vertical
            return predicted

        predicted = predict(range(kernels // 4), [jnp.zeros((block, WINDOW), jnp.float32)] * 2)
        for part in range(2):
            resid[pl.ds(part * block, block), cols] = predicted[part]
        for more in range(1, per + 1):
            @pl.when((step + 1) * per + more < count)
            def _():
                take_block((step + 1) * per + more)
        predicted = [resid[pl.ds(part * block, block), cols] for part in range(2)]
        predicted = predict(range(kernels // 4, kernels // 2), predicted)
        for part in range(2):
            rows = pl.ds(part * block, block)
            mask = usable[rows, :].astype(jnp.float32)
            mask = jnp.concatenate([mask] * per, axis=1)
            resid[rows, cols] = mask * (predicted[part] - seen[rows, cols].astype(jnp.float32))
        res_ref[:, cols] = resid[pl.ds(inner, strip), cols]

    def term_copy(b):
        return pltpu.make_async_remote_copy(
            src_ref=leaving.at[b], dst_ref=arrived.at[me],
            send_sem=term_send.at[b], recv_sem=term_recv.at[me],
            device_id={"exp": b}, device_id_type=MESH)

    lane_side = lax.broadcasted_iota(jnp.int32, (strip, LANES), 1) // (LANES // 2)

    def send_term(rank):
        b = reversed_order(rank, count)
        c, side = b // per, b % per
        beside = stray[jnp.where(side == 0, c, c + 2)]
        term = tot[:, lane_block(b)] + jnp.where(lane_side == side, beside, 0.0)
        leaving[b] = term.astype(leaving.dtype)

        @pl.when(b != me)
        def _():
            term_copy(b).start()

    @pl.loop(0, chunks)
    def _(step):
        c = reversed_order(step, chunks)
        cols = chunk_cols(c)
        inside = jnp.zeros((strip, WINDOW), jnp.float32)
        outside = jnp.zeros((strip, LANES), jnp.float32)
        left = lax.broadcasted_iota(jnp.int32, (strip, LANES), 1) < LANES // 2
        for pair in range(kernels // 2):
            edges = []
            for odd in range(2):
                k = 2 * pair + odd
                weighted = (coef[k, :, cols].astype(jnp.float32) * resid[:, cols]).astype(jnp.bfloat16)
                back = jnp.concatenate([
                    jnp.dot(
                        bw[k, part], weighted[part * low_b:part * low_b + WINDOW],
                        preferred_element_type=jnp.float32).astype(jnp.bfloat16)
                    for part in range(2)], axis=0)
                inside += jnp.dot(back, gw[k], preferred_element_type=jnp.float32)
                edges.append(jnp.where(left, back[:, :LANES], back[:, LANES:]))
            outside += jnp.dot(
                jnp.concatenate(edges, axis=1), ew[pair], preferred_element_type=jnp.float32)
        tot[:, cols] = inside
        stray[c + 1] = outside

        @pl.when(step > 0)
        def _():
            send_term(step * per - 1)

        send_term(step * per)

    send_term(count - 1)

    for c in range(grad_ref.shape[0]):
        grad_ref[c] = jnp.where(owned(me, c), leaving[me].astype(jnp.float32), 0.0)
    for rank in range(count):
        e = reversed_order(rank, count)

        @pl.when(e != me)
        def _():
            pltpu.make_async_copy(leaving.at[0], arrived.at[e], term_recv.at[e]).wait()
            value = arrived[e].astype(jnp.float32)
            for c in range(grad_ref.shape[0]):
                grad_ref[c] += jnp.where(owned(e, c), value, 0.0)

    for e in range(count):
        @pl.when(e != me)
        def _():
            lat_copy(e).wait_send()
            term_copy(e).wait_send()
    for side, there in sends:
        @pl.when(there)
        def _():
            for copy in seen_copies(side):
                copy.wait_send()
            for c in range(chunks):
                halo_copies(c, side).wait_send()
            for b in range(count):
                rim_copy(b, side).wait_send()


def fused_body(latent, row_taps, column_taps, coefficients, observed, cell_of, valid_rows):
    kernels, tap_count = row_taps.shape
    half_width = tap_count // 2
    strip, width = observed.shape[1:]
    ncells = latent.shape[0]
    inner = round_up(half_width, PACK)
    outer = round_up(2 * half_width, PACK)
    count, row_count = lax.axis_size("exp"), lax.axis_size("row")

    vmem = pl.BlockSpec(memory_space=pltpu.VMEM)
    hbm = pl.BlockSpec(memory_space=pltpu.HBM)
    chunks = width // WINDOW
    block = strip // 2 + inner
    bf16 = jnp.bfloat16
    dma = pltpu.SemaphoreType.DMA
    dims = (count, row_count, kernels, tap_count, strip, width, inner, outer)
    residual, gradient = pl.pallas_call(
        functools.partial(fused_kernel, dims),
        out_shape=(
            jax.ShapeDtypeStruct((strip, width), jnp.float32),
            jax.ShapeDtypeStruct((ncells, strip, LANES), jnp.float32),
        ),
        in_specs=[hbm] * 7,
        out_specs=(vmem, vmem),
        scratch_shapes=[
            pltpu.VMEM((1, count), jnp.int32),
            pltpu.VMEM((ncells, strip, LANES), bf16),
            pltpu.VMEM((kernels, tap_count), bf16),
            pltpu.VMEM((kernels, tap_count), bf16),
            pltpu.VMEM((1, strip), jnp.int32),
            pltpu.VMEM((count, 8, LANES), jnp.int32),
            pltpu.VMEM((4, kernels, WINDOW), jnp.float32),
            pltpu.VMEM((kernels, strip + 2 * inner, width), bf16),
            pltpu.VMEM((strip + 2 * inner, width), bf16),
            pltpu.VMEM((strip + 2 * inner, LANES), bf16),
            pltpu.VMEM((count, strip, LANES), bf16),
            pltpu.VMEM((strip + 2 * outer, width + 2 * LANES), bf16),
            pltpu.VMEM((strip + 2 * outer, WINDOW + LANES), bf16),
            pltpu.VMEM((kernels // 2, WINDOW, 2 * LANES), bf16),
            pltpu.VMEM((kernels, WINDOW, WINDOW), bf16),
            pltpu.VMEM((kernels // 2, WINDOW, LANES), bf16),
            pltpu.VMEM((kernels, 2, block, WINDOW), bf16),
            pltpu.VMEM((kernels, 2, strip // 2, WINDOW), bf16),
            pltpu.VMEM((strip + 2 * inner, width), jnp.float32),
            pltpu.VMEM((strip, width), jnp.float32),
            pltpu.VMEM((chunks + 2, strip, LANES), jnp.float32),
            pltpu.VMEM((count, strip, LANES), bf16),
            pltpu.VMEM((count, strip, LANES), bf16),
            dma((chunks + 6,)),
            dma((count,)), dma((count,)),
            dma((2, count)), dma((2, count)),
            dma((2, chunks + 2)), dma((2, chunks + 2)),
            dma((count,)), dma((count,)),
        ],
        compiler_params=pltpu.CompilerParams(
            vmem_limit_bytes=44 * 2**20, collective_id=0, has_side_effects=True),
        cost_estimate=pl.CostEstimate(flops=10**10, bytes_accessed=2 * 10**7, transcendentals=0),
    )(*[pltpu.with_memory_space_constraint(x, pltpu.HBM) for x in (
        cell_of.reshape(1, count), latent, row_taps, column_taps, valid_rows, observed[0], coefficients[0])])
    return (gradient, residual[None])


def body(latent, *others):
    if latent.shape[2] == LANES:
        return fused_body(latent, *others)
    return apart_body(latent, *others)


def solution(mesh):
    placed = (
        P(None, "row", "exp"),
        P(),
        P(),
        P("exp", None, "row", None),
        P("exp", "row", None),
        P(),
        P("exp", "row"),
    )
    return jax.shard_map(
        body,
        mesh=mesh,
        in_specs=placed,
        out_specs=(P(None, "row", "exp"), P("exp", "row", None)),
        check_vma=False,
    )
```

profile of v0, /device:TPU:0, one launch (start us, length us, event | category | flops | bytes accessed | tf_op | source)
XLA Modules:
  0.0 52.7 jit_solution(2646442637456416883)
XLA Ops:
  0.6 50.3 %shard_map.86 = (f32[256,1024]{1,0:T(8,128)S(1)}, f32[4,256,128]{2,1,0:T(8,128)S(1)}) custom-call(s32[1,8]{1,0:T(1,128)} %bitcast.7, bf16[4,256,128]{2,1,0:T(8,128)(2,1)} %lat_hbm.1, bf16[16,21]{1,0:T(8,128)(2,1)} %along_hbm.1, bf16[16,21]{1,0:T(8,128)(2,1)} %down_hbm.1, s32[1,256]{1,0:T(1,128)} %valid_hbm.1, bf16[256,1024]{1,0:T(8,128)(2,1)} %bitcast.6, ...), custom_call_target="tpu_custom_call" | custom-call | flops 10000000000 | bytes 20000000 | tf_op jit(solution)/shard_map/pallas_call | solution.py:585
  51.0 0.8 %copy.11 = f32[4,256,128]{2,1,0:T(8,128)} copy(f32[4,256,128]{2,1,0:T(8,128)S(1)} %get-tuple-element.8) | data formatting | bytes 1048576
  51.8 1.0 %copy.12 = f32[1,256,1024]{2,1,0:T(8,128)} copy(f32[1,256,1024]{2,1,0:T(8,128)S(1)} %bitcast.4) | data formatting | bytes 2097152
where the time goes:
time: 52.9 us; the launch traced here: 52.7 us
  Pallas kernels  50.3 us (95%)
  local copies, waits for them, and re-layouts  1.77 us (3%)
  between operations  0.64 us (1%)
    pallas_call x1, Pallas kernels, fused_body(): pl.pallas_call(functools.partial(fused_kernel, dims), out_shape=(jax.Shap...  50.3 us
    unnamed x2, local copies, waits for them, and re-layouts  1.77 us

commit v1 on v0

--- a/solution.py
+++ b/solution.py
@@ -204,7 +204,7 @@
     dims,
     cells_hbm, lat_hbm, along_hbm, down_hbm, valid_hbm, obs_hbm, coef_hbm,
     res_ref, grad_ref,
-    cells_ref, lat_ref, along_ref, down_ref, valid_ref, cells, taps_ref, coef, seen, usable, outgoing, lat, lsh, fw, gw, ew, aw, bw, resid, tot, stray, leaving, arrived,
+    cells_ref, lat_ref, along_ref, down_ref, valid_ref, cells, taps_ref, coef, seen, usable, outgoing, lat, lsh, fw, gw, ew, aw, bw, rb, resid, tot, stray, leaving, arrived,
     own_sems, lat_send, lat_recv, rim_send, rim_recv, halo_send, halo_recv, term_send, term_recv,
 ):
     count, row_count, kernels, tap_count, strip, width, inner, outer = dims
@@ -447,44 +447,32 @@
                 take_rims(step * per + more)
         near = lat[:, pl.ds(pl.multiple_of(c * WINDOW, WINDOW), WINDOW + 2 * LANES)]
         lsh[...] = near[:, LANES // 2:LANES // 2 + WINDOW + LANES]
+        for b in range(per):
+            window = lsh[:, pl.ds(b * LANES, WINDOW)]
+            for pair in range(kernels // 2):
+                both = jnp.dot(window, fw[pair], preferred_element_type=jnp.float32).astype(rb.dtype)
+                rb[2 * pair, :, pl.ds(b * LANES, LANES)] = both[:, :LANES]
+                rb[2 * pair + 1, :, pl.ds(b * LANES, LANES)] = both[:, LANES:]
         own_coef(c).wait()
         for side, there in receives:
             @pl.when(there)
             def _():
                 halo_copies(c, side).wait_recv()
-        windows = [lsh[:, b * LANES:b * LANES + WINDOW] for b in range(per)]
-
-        def predict(pairs, predicted):
-            for pair in pairs:
-                both = [
-                    jnp.dot(window, fw[pair], preferred_element_type=jnp.float32).astype(jnp.bfloat16)
-                    for window in windows]
-                for odd in range(2):
-                    k = 2 * pair + odd
-                    blurred = jnp.concatenate(
-                        [found[:, odd * LANES:(odd + 1) * LANES] for found in both], axis=1)
-                    for part in range(2):
-                        vertical = jnp.dot(
-                            aw[k, part], blurred[part * low_a:part * low_a + WINDOW],
-                            preferred_element_type=jnp.float32)
-                        gain = coef[k, pl.ds(part * block, block), cols].astype(jnp.float32)
-                        predicted[part] = predicted[part] + gain * vertical
-            return predicted
-
-        predicted = predict(range(kernels // 4), [jnp.zeros((block, WINDOW), jnp.float32)] * 2)
         for part in range(2):
-            resid[pl.ds(part * block, block), cols] = predicted[part]
-        for more in range(1, per + 1):
-            @pl.when((step + 1) * per + more < count)
-            def _():
-                take_block((step + 1) * per + more)
-        predicted = [resid[pl.ds(part * block, block), cols] for part in range(2)]
-        predicted = predict(range(kernels // 4, kernels // 2), predicted)
-        for part in range(2):
+            if part == 1:
+                for more in range(1, per + 1):
+                    @pl.when((step + 1) * per + more < count)
+                    def _():
+                        take_block((step + 1) * per + more)
             rows = pl.ds(part * block, block)
+            reach = pl.ds(part * low_a, WINDOW)
+            predicted = jnp.zeros((block, WINDOW), jnp.float32)
+            for k in range(kernels):
+                vertical = jnp.dot(aw[k, part], rb[k, reach, :], preferred_element_type=jnp.float32)
+                predicted += coef[k, rows, cols].astype(jnp.float32) * vertical
             mask = usable[rows, :].astype(jnp.float32)
             mask = jnp.concatenate([mask] * per, axis=1)
-            resid[rows, cols] = mask * (predicted[part] - seen[rows, cols].astype(jnp.float32))
+            resid[rows, cols] = mask * (predicted - seen[rows, cols].astype(jnp.float32))
         res_ref[:, cols] = resid[pl.ds(inner, strip), cols]
 
     def term_copy(b):
@@ -609,6 +597,7 @@
             pltpu.VMEM((kernels // 2, WINDOW, LANES), bf16),
             pltpu.VMEM((kernels, 2, block, WINDOW), bf16),
             pltpu.VMEM((kernels, 2, strip // 2, WINDOW), bf16),
+            pltpu.VMEM((kernels, strip + 2 * outer, WINDOW), bf16),
             pltpu.VMEM((strip + 2 * inner, width), jnp.float32),
             pltpu.VMEM((strip, width), jnp.float32),
             pltpu.VMEM((chunks + 2, strip, LANES), jnp.float32),

time: 52.9 us -> 51.7 us (0.977)
  Pallas kernels: 50.3 us -> 49.2 us
    pallas_call x1, Pallas kernels: 50.3 us -> 49.2 us  [fused_body(): pl.pallas_call(functools.partial(fused_kernel, dims), out_shape=(jax.Shap...]
where the time goes in v1:
time: 51.7 us; the launch traced here: 51.6 us
  Pallas kernels  49.2 us (95%)
  local copies, waits for them, and re-layouts  1.77 us (3%)
  between operations  0.64 us (1%)
    pallas_call x1, Pallas kernels, fused_body(): pl.pallas_call(functools.partial(fused_kernel, dims), out_shape=(jax.Shap...  49.2 us
    unnamed x2, local copies, waits for them, and re-layouts  1.77 us

profile of v1, /device:TPU:0, one launch (start us, length us, event | category | flops | bytes accessed | tf_op | source)
XLA Modules:
  0.0 51.6 jit_solution(8636471603966410887)
XLA Ops:
  0.6 49.2 %shard_map.86 = (f32[256,1024]{1,0:T(8,128)S(1)}, f32[4,256,128]{2,1,0:T(8,128)S(1)}) custom-call(s32[1,8]{1,0:T(1,128)} %bitcast.7, bf16[4,256,128]{2,1,0:T(8,128)(2,1)} %lat_hbm.1, bf16[16,21]{1,0:T(8,128)(2,1)} %along_hbm.1, bf16[16,21]{1,0:T(8,128)(2,1)} %down_hbm.1, s32[1,256]{1,0:T(1,128)} %valid_hbm.1, bf16[256,1024]{1,0:T(8,128)(2,1)} %bitcast.6, ...), custom_call_target="tpu_custom_call" | custom-call | flops 10000000000 | bytes 20000000 | tf_op jit(solution)/shard_map/pallas_call | solution.py:573
  49.8 0.8 %copy.11 = f32[4,256,128]{2,1,0:T(8,128)} copy(f32[4,256,128]{2,1,0:T(8,128)S(1)} %get-tuple-element.8) | data formatting | bytes 1048576
  50.6 1.0 %copy.12 = f32[1,256,1024]{2,1,0:T(8,128)} copy(f32[1,256,1024]{2,1,0:T(8,128)S(1)} %bitcast.4) | data formatting | bytes 2097152

commit v2 on v1

--- a/solution.py
+++ b/solution.py
@@ -11,6 +11,7 @@
 WINDOW = 256
 PACK = 16
 STEP = 64
+GROUP = 4
 MESH = pl.DeviceIdType.MESH
 
 
@@ -501,20 +502,26 @@
         inside = jnp.zeros((strip, WINDOW), jnp.float32)
         outside = jnp.zeros((strip, LANES), jnp.float32)
         left = lax.broadcasted_iota(jnp.int32, (strip, LANES), 1) < LANES // 2
-        for pair in range(kernels // 2):
-            edges = []
-            for odd in range(2):
-                k = 2 * pair + odd
+        for group in range(kernels // GROUP):
+            backs, edges = [], []
+            for odd in range(GROUP):
+                k = GROUP * group + odd
                 weighted = (coef[k, :, cols].astype(jnp.float32) * resid[:, cols]).astype(jnp.bfloat16)
                 back = jnp.concatenate([
                     jnp.dot(
                         bw[k, part], weighted[part * low_b:part * low_b + WINDOW],
                         preferred_element_type=jnp.float32).astype(jnp.bfloat16)
                     for part in range(2)], axis=0)
-                inside += jnp.dot(back, gw[k], preferred_element_type=jnp.float32)
+                backs.append(back)
                 edges.append(jnp.where(left, back[:, :LANES], back[:, LANES:]))
+            inside += jnp.dot(
+                jnp.concatenate(backs, axis=1),
+                gw[GROUP * group:GROUP * (group + 1)].reshape(GROUP * WINDOW, WINDOW),
+                preferred_element_type=jnp.float32)
             outside += jnp.dot(
-                jnp.concatenate(edges, axis=1), ew[pair], preferred_element_type=jnp.float32)
+                jnp.concatenate(edges, axis=1),
+                ew[GROUP // 2 * group:GROUP // 2 * (group + 1)].reshape(GROUP * LANES, LANES),
+                preferred_element_type=jnp.float32)
         tot[:, cols] = inside
         stray[c + 1] = outside
 

time: 51.7 us -> 50.1 us (0.969)
  Pallas kernels: 49.2 us -> 47.5 us
    pallas_call x1, Pallas kernels: 49.2 us -> 47.5 us  [fused_body(): pl.pallas_call(functools.partial(fused_kernel, dims), out_shape=(jax.Shap...]
where the time goes in v2:
time: 50.1 us; the launch traced here: 49.9 us
  Pallas kernels  47.5 us (95%)
  local copies, waits for them, and re-layouts  1.77 us (4%)
  between operations  0.64 us (1%)
    pallas_call x1, Pallas kernels, fused_body(): pl.pallas_call(functools.partial(fused_kernel, dims), out_shape=(jax.Shap...  47.5 us
    unnamed x2, local copies, waits for them, and re-layouts  1.77 us

profile of v2, /device:TPU:0, one launch (start us, length us, event | category | flops | bytes accessed | tf_op | source)
XLA Modules:
  0.0 49.9 jit_solution(4963791700231198964)
XLA Ops:
  0.6 47.5 %shard_map.86 = (f32[256,1024]{1,0:T(8,128)S(1)}, f32[4,256,128]{2,1,0:T(8,128)S(1)}) custom-call(s32[1,8]{1,0:T(1,128)} %bitcast.7, bf16[4,256,128]{2,1,0:T(8,128)(2,1)} %lat_hbm.1, bf16[16,21]{1,0:T(8,128)(2,1)} %along_hbm.1, bf16[16,21]{1,0:T(8,128)(2,1)} %down_hbm.1, s32[1,256]{1,0:T(1,128)} %valid_hbm.1, bf16[256,1024]{1,0:T(8,128)(2,1)} %bitcast.6, ...), custom_call_target="tpu_custom_call" | custom-call | flops 10000000000 | bytes 20000000 | tf_op jit(solution)/shard_map/pallas_call | solution.py:580
  48.2 0.8 %copy.11 = f32[4,256,128]{2,1,0:T(8,128)} copy(f32[4,256,128]{2,1,0:T(8,128)S(1)} %get-tuple-element.8) | data formatting | bytes 1048576
  49.0 1.0 %copy.12 = f32[1,256,1024]{2,1,0:T(8,128)} copy(f32[1,256,1024]{2,1,0:T(8,128)S(1)} %bitcast.4) | data formatting | bytes 2097152

commit v3 on v2

--- a/solution.py
+++ b/solution.py
@@ -11,7 +11,7 @@
 WINDOW = 256
 PACK = 16
 STEP = 64
-GROUP = 4
+GROUP = 8
 MESH = pl.DeviceIdType.MESH
 
 

time: 50.1 us -> 50.1 us (level)
  no operation moved by 1% of the time
where the time goes in v3:
time: 50.1 us; the launch traced here: 49.9 us
  Pallas kernels  47.5 us (95%)
  local copies, waits for them, and re-layouts  1.77 us (4%)
  between operations  0.64 us (1%)
    pallas_call x1, Pallas kernels, fused_body(): pl.pallas_call(functools.partial(fused_kernel, dims), out_shape=(jax.Shap...  47.5 us
    unnamed x2, local copies, waits for them, and re-layouts  1.77 us

profile of v3, /device:TPU:0, one launch (start us, length us, event | category | flops | bytes accessed | tf_op | source)
XLA Modules:
  0.0 49.9 jit_solution(14061653535697834688)
XLA Ops:
  0.6 47.5 %shard_map.86 = (f32[256,1024]{1,0:T(8,128)S(1)}, f32[4,256,128]{2,1,0:T(8,128)S(1)}) custom-call(s32[1,8]{1,0:T(1,128)} %bitcast.7, bf16[4,256,128]{2,1,0:T(8,128)(2,1)} %lat_hbm.1, bf16[16,21]{1,0:T(8,128)(2,1)} %along_hbm.1, bf16[16,21]{1,0:T(8,128)(2,1)} %down_hbm.1, s32[1,256]{1,0:T(1,128)} %valid_hbm.1, bf16[256,1024]{1,0:T(8,128)(2,1)} %bitcast.6, ...), custom_call_target="tpu_custom_call" | custom-call | flops 10000000000 | bytes 20000000 | tf_op jit(solution)/shard_map/pallas_call | solution.py:580
  48.2 0.8 %copy.11 = f32[4,256,128]{2,1,0:T(8,128)} copy(f32[4,256,128]{2,1,0:T(8,128)S(1)} %get-tuple-element.8) | data formatting | bytes 1048576
  49.0 1.0 %copy.12 = f32[1,256,1024]{2,1,0:T(8,128)} copy(f32[1,256,1024]{2,1,0:T(8,128)S(1)} %bitcast.4) | data formatting | bytes 2097152
